TPU v7x, 512 devices: a whole 4x4x16 slice. The times are simulated.
512 devices in a mesh: ctx: 128 (over z, x, core), tp: 4 (over y).
Axes of the slice: x: 4, y: 4, z: 16, core: 2. Of those that a mesh axis runs over, the one named last changes fastest.
Arguments:
- queries: bfloat16 [32768, 1024], P('ctx', 'tp'), may hold values from -6 to 6
- keys: bfloat16 [32768, 1024], P('ctx', 'tp'), may hold values from -6 to 6
- values: bfloat16 [32768, 1024], P('ctx', 'tp'), may hold values from -20 to 20, as said below
- gain: float32 [1024], P('tp'), may hold values from 0.25 to 1.75
- out_grad: bfloat16 [32768, 1024], P('ctx', 'tp'), may hold values from -6 to 6
Outputs:
- normed: bfloat16 [32768, 1024], P('ctx', 'tp')
- grad_queries: bfloat16 [32768, 1024], P('ctx', 'tp')
- grad_keys: bfloat16 [32768, 1024], P('ctx', 'tp')
- grad_values: bfloat16 [32768, 1024], P('ctx', 'tp')
Inputs may be any that keep to these rules, and one draw needn't show every extreme that they name: values of order one, each head at its own scale.
All inputs are finite; a program needn't handle non-finite values.
Results may differ from a plain program's by a relative error of at most 0.0065.
Values sent between devices are 32-bit elements; how exact they have to be, the bound alone decides.
A program may use at most 64 MiB of HBM per device.

v0:
```python
import jax
import jax.numpy as jnp
from jax import lax
from jax.sharding import PartitionSpec as P

HEAD = 128


epsilon = 1e-06


def carried_in(part, axis, combine, identity, reverse):
    count = lax.axis_size(axis)
    place = lax.axis_index(axis)
    ahead = count - 1 - place if reverse else place
    gathered = lax.all_gather(part, axis)
    state = jnp.zeros_like(part) + jnp.asarray(identity, part.dtype)

    def one(lap, state):
        source = count - 1 - lap if reverse else lap
        return combine(state, lax.dynamic_index_in_dim(gathered, source, 0, False))

    return lax.fori_loop(0, ahead, one, state)


def add_terms(earlier, later):
    return earlier + later


def on_device(queries, keys, values, gain, out_grad):
    tokens = queries.shape[0]
    local_width = queries.shape[1]
    head_count = local_width // HEAD
    chain_len = lax.axis_size("ctx")
    factor = (HEAD * tokens * chain_len) ** (-0.5)
    features = local_width * lax.axis_size("tp")
    q_blk = queries.reshape(tokens, head_count, HEAD)
    k_blk = keys.reshape(tokens, head_count, HEAD)
    v_blk = values.reshape(tokens, head_count, HEAD)
    position = jnp.arange(tokens, dtype=jnp.int32)
    causal = position[:, None] >= position[None, :]
    states = jnp.einsum("thd,the->hde", k_blk, v_blk, preferred_element_type=jnp.float32)
    prefix_sum = carried_in(states, "ctx", add_terms, jnp.zeros_like(states), False)
    prefix = prefix_sum.astype(jnp.bfloat16)
    raw = jnp.einsum("thd,shd->hts", q_blk, k_blk, preferred_element_type=jnp.float32) * factor
    scores = jnp.where(causal[None], raw, 0.0).astype(jnp.bfloat16)
    attended = factor * jnp.einsum(
        "thd,hde->the", q_blk, prefix, preferred_element_type=jnp.float32
    )
    attended = attended + jnp.einsum(
        "hts,she->the", scores, v_blk, preferred_element_type=jnp.float32
    )
    power = lax.psum(jnp.sum(attended * attended, axis=(1, 2)), "tp")
    inv_rms = lax.rsqrt(power / features + epsilon)
    gains = gain.reshape(head_count, HEAD)
    normed = (
        (attended * inv_rms[:, None, None] * gains)
        .reshape(tokens, local_width)
        .astype(jnp.bfloat16)
    )
    weighted = out_grad.astype(jnp.float32).reshape(tokens, head_count, HEAD) * gains
    row_total = lax.psum(jnp.sum(weighted * attended, axis=(1, 2)), "tp")
    row_mean = row_total / features
    grad_attn = inv_rms[:, None, None] * (
        weighted - attended * (inv_rms * inv_rms * row_mean)[:, None, None]
    )
    grad_attn = grad_attn.astype(jnp.bfloat16)
    updates = jnp.einsum("thd,the->hde", q_blk, grad_attn, preferred_element_type=jnp.float32)
    suffix_sum = carried_in(updates, "ctx", add_terms, jnp.zeros_like(updates), True)
    suffix = suffix_sum.astype(jnp.bfloat16)
    raw_grad = (
        jnp.einsum("the,she->hts", grad_attn, v_blk, preferred_element_type=jnp.float32) * factor
    )
    grad_scores = jnp.where(causal[None], raw_grad, 0.0).astype(jnp.bfloat16)
    grad_q = factor * jnp.einsum(
        "the,hde->thd", grad_attn, prefix, preferred_element_type=jnp.float32
    )
    grad_q = grad_q + jnp.einsum(
        "hts,shd->thd", grad_scores, k_blk, preferred_element_type=jnp.float32
    )
    grad_k = factor * jnp.einsum("the,hde->thd", v_blk, suffix, preferred_element_type=jnp.float32)
    grad_k = grad_k + jnp.einsum(
        "hts,thd->shd", grad_scores, q_blk, preferred_element_type=jnp.float32
    )
    grad_v = factor * jnp.einsum("thd,hde->the", k_blk, suffix, preferred_element_type=jnp.float32)
    grad_v = grad_v + jnp.einsum(
        "hts,the->she", scores, grad_attn, preferred_element_type=jnp.float32
    )
    return (
        normed,
        grad_q.reshape(tokens, local_width).astype(jnp.bfloat16),
        grad_k.reshape(tokens, local_width).astype(jnp.bfloat16),
        grad_v.reshape(tokens, local_width).astype(jnp.bfloat16),
    )


def solution(mesh):
    placed = (P("ctx", "tp"), P("ctx", "tp"), P("ctx", "tp"), P("tp"), P("ctx", "tp"))
    return jax.shard_map(
        on_device,
        mesh=mesh,
        in_specs=placed,
        out_specs=(P("ctx", "tp"), P("ctx", "tp"), P("ctx", "tp"), P("ctx", "tp")),
        check_vma=False,
    )
```

profile of v0, /device:TPU:1, one launch (start us, length us, event | category | flops | bytes accessed | tf_op | source)
XLA Modules:
  0.0 588.3 jit_solution(5190904574070878853)
XLA Ops:
  7.2 1.0 copy.84
  9.2 1.0 copy.57
  10.2 1.0 copy.38
  11.2 1.2 fusion.2
  12.4 163.3 %all-gather.5.cloned.1.call-done = f32[256,128,128]{2,1,0:T(8,128)} async-done(((f32[2,128,128]{2,1,0:T(8,128)}), f32[256,128,128]{2,1,0:T(8,128)}) %all-gather.5.cloned.1.call-update) | async-done | bytes 16777232 | tf_op jit(solution)/shard_map/all_gather | solution.py:16
  175.8 1.0 while.22
  175.8 0.9 bitcast_add_fusion.4
  177.0 0.9 multiply_reduce_fusion
  177.9 8.5 %all-reduce = (f32[256]{0:T(256)S(1)}, f32[256]{0:T(256)S(1)}) all-reduce(f32[256]{0:T(256)S(1)} %get-tuple-element.98, f32[256]{0:T(256)S(1)} %get-tuple-element.97), channel_id=1, replica_groups=mesh['ctx'=128,'tp'=4] {'tp'}, use_global_device_ids=true, to_apply=%region_3.4 | all-reduce | flops 512 | bytes 4096 | tf_op jit(solution)/shard_map/psum | solution.py:53
  190.4 266.9 %all-gather.7.cloned.1.call-done = f32[256,128,128]{2,1,0:T(8,128)} async-done(((f32[2,128,128]{2,1,0:T(8,128)}), f32[256,128,128]{2,1,0:T(8,128)}) %all-gather.7.cloned.1.call-update) | async-done | bytes 16777232 | tf_op jit(solution)/shard_map/all_gather | solution.py:16
  457.3 120.9 %while.23 = (s32[]{:T(128)}, f32[2,128,128]{2,1,0:T(8,128)S(1)}, s32[]{:T(128)}, f32[128,2,128,128]{3,2,1,0:T(8,128)}, s32[]{:T(128)}, /*index=5*/s32[]{:T(128)}, s32[]{:T(128)}, s32[]{:T(128)}) while((s32[]{:T(128)}, f32[2,128,128]{2,1,0:T(8,128)S(1)}, s32[]{:T(128)}, f32[128,2,128,128]{3,2,1,0:T(8,128)}, s32[]{:T(128)}, ...), condition=%wide.region_7.8_spmd, body=%wide.region_6.7_spmd.sunk | while | flops 32774 | bytes 393359 | solution.py:23
  457.3 0.9 bitcast_add_fusion.5
  458.3 0.9 bitcast_add_fusion.5
  459.2 0.9 bitcast_add_fusion.5
  460.2 0.9 bitcast_add_fusion.5
  461.2 0.9 bitcast_add_fusion.5
  462.1 0.9 bitcast_add_fusion.5
  463.1 0.9 bitcast_add_fusion.5
  464.0 0.9 bitcast_add_fusion.5
  465.0 0.9 bitcast_add_fusion.5
  466.0 0.9 bitcast_add_fusion.5
  466.9 0.9 bitcast_add_fusion.5
  467.9 0.9 bitcast_add_fusion.5
  468.8 0.9 bitcast_add_fusion.5
  469.8 0.9 bitcast_add_fusion.5
  470.8 0.9 bitcast_add_fusion.5
  471.7 0.9 bitcast_add_fusion.5
  472.7 0.9 bitcast_add_fusion.5
  473.6 0.9 bitcast_add_fusion.5
  474.6 0.9 bitcast_add_fusion.5
  475.6 0.9 bitcast_add_fusion.5
  476.5 0.9 bitcast_add_fusion.5
  477.5 0.9 bitcast_add_fusion.5
  478.4 0.9 bitcast_add_fusion.5
  479.4 0.9 bitcast_add_fusion.5
  480.4 0.9 bitcast_add_fusion.5
  481.3 0.9 bitcast_add_fusion.5
  482.3 0.9 bitcast_add_fusion.5
  483.2 0.9 bitcast_add_fusion.5
  484.2 0.9 bitcast_add_fusion.5
  485.2 0.9 bitcast_add_fusion.5
  486.1 0.9 bitcast_add_fusion.5
  487.1 0.9 bitcast_add_fusion.5
  488.0 0.9 bitcast_add_fusion.5
  489.0 0.9 bitcast_add_fusion.5
  490.0 0.9 bitcast_add_fusion.5
  490.9 0.9 bitcast_add_fusion.5
  491.9 0.9 bitcast_add_fusion.5
  492.8 0.9 bitcast_add_fusion.5
  493.8 0.9 bitcast_add_fusion.5
  494.8 0.9 bitcast_add_fusion.5
  495.7 0.9 bitcast_add_fusion.5
  496.7 0.9 bitcast_add_fusion.5
  498.6 0.9 bitcast_add_fusion.5
  501.5 0.9 bitcast_add_fusion.5
  516.8 0.9 bitcast_add_fusion.5
  519.7 0.9 bitcast_add_fusion.5
  535.0 0.9 bitcast_add_fusion.5
  537.9 0.9 bitcast_add_fusion.5
  553.3 0.9 bitcast_add_fusion.5
  556.2 0.9 bitcast_add_fusion.5
  571.5 0.9 bitcast_add_fusion.5
  574.4 0.9 bitcast_add_fusion.5
  578.4 1.1 convolution_multiply_fusion.2
  (99 shorter events, 76.6 us)
Async XLA Ops:
  7.2 1.1 copy-start
  7.2 168.6 %all-gather.5.cloned.1.call-start = ((), (), s32[]{:S(2)}) async-start(), calls=%async_computation | async-start | bytes 16908288 | tf_op jit(solution)/shard_map/all_gather | solution.py:16
  9.1 448.2 %all-gather.7.cloned.1.call-start = ((), (), s32[]{:S(2)}) async-start(), calls=%async_computation.1 | async-start | bytes 16908288 | tf_op jit(solution)/shard_map/all_gather | solution.py:16
Sparse Core Ops, SparseCore 0:
  11.7 163.9 all-gather.4
  188.4 268.8 all-gather.6
where the time goes:
time: 591 us; the launch traced here: 588 us
  waiting for transfers between devices  430 us (73%)
  other arithmetic  120 us (20%)
  between operations  14.2 us (2%)
  blocking collectives  8.51 us (1%)
  local copies, waits for them, and re-layouts  6.87 us (1%)
    all_gather x2, waiting for transfers between devices, carried_in(): gathered = lax.all_gather(part, axis)  430 us
    add x127, other arithmetic, add_terms(): return earlier + later  119 us
  transfers between devices with their start and end apart: 2, of which 2 were waited for; matrix products, arithmetic and copies ran while one was open for 1% of the time, Pallas kernels for 0%

commit v1 on v0

v1 whole, which is shorter than its diff:
```python
import functools

import jax
import jax.numpy as jnp
from jax import lax
from jax.experimental import pallas as pl
from jax.experimental.pallas import tpu as pltpu
from jax.sharding import PartitionSpec as P

HEAD = 128
GROUP = 16
EPSILON = 1e-06
MESH = pl.DeviceIdType.MESH
F32 = jnp.float32
BF16 = jnp.bfloat16

STEPS = sorted(
    [(dz, dx, dc) for dz in range(2) for dx in range(4) for dc in range(2) if (dz, dx, dc) != (0, 0, 0)],
    key=lambda s: -(s[0] + min(s[1], 4 - s[1]) + 0.1 * s[2]),
)


def dot(a, b):
    return lax.dot_general(a, b, (((1,), (0,)), ((), ())), preferred_element_type=F32)


def dot_t(a, b):
    return lax.dot_general(a, b, (((1,), (1,)), ((), ())), preferred_element_type=F32)


def core_kernel(
    n_ctx, n_tp,
    q_hbm, k_hbm, v_hbm, gain_ref, og_hbm,
    normed_hbm, gq_hbm, gk_hbm, gv_hbm,
    q, k, v, og,
    part, got, total, others, before, scan_out,
    rows_out, rows_in,
    q_t, v_t, w_t, local_t, att_t, scores_t, ga_t,
    gk_part, gv_part, obuf,
    in_sem, out_sem, send1, recv1, send2, recv2, send3, recv3, send_tp, recv_tp,
):
    ctx = lax.axis_index("ctx")
    tp = lax.axis_index("tp")
    n_groups = n_ctx // GROUP
    group = ctx // GROUP
    member = ctx % GROUP
    half, x, core = member // 8, (member // 2) % 4, member % 2
    tokens, width = q.shape
    heads = width // HEAD
    slice_rows = part.shape[2]
    factor = (HEAD * tokens * n_ctx) ** (-0.5)
    features = width * n_tp

    loads = [
        pltpu.make_async_copy(src, dst, in_sem.at[i])
        for i, (src, dst) in enumerate(((k_hbm, k), (v_hbm, v), (q_hbm, q), (og_hbm, og)))
    ]
    for load in loads:
        load.start()
    others[...] = jnp.zeros_like(others)

    def member_at(step):
        dz, dx, dc = step
        return ((half + dz) % 2) * 8 + ((x + dx) % 4) * 2 + (core + dc) % 2

    barrier = pltpu.get_barrier_semaphore()
    for d in range(1, n_groups):
        pl.semaphore_signal(
            barrier, inc=1, device_id=(((group + d) % n_groups) * GROUP + member, tp), device_id_type=MESH
        )
    for step in STEPS:
        pl.semaphore_signal(
            barrier, inc=1, device_id=(group * GROUP + member_at(step), tp), device_id_type=MESH
        )
    for d in range(1, n_tp):
        pl.semaphore_signal(barrier, inc=1, device_id=(ctx, (tp + d) % n_tp), device_id_type=MESH)

    row = lax.broadcasted_iota(jnp.int32, (tokens, tokens), 0)
    col = lax.broadcasted_iota(jnp.int32, (tokens, tokens), 1)
    causal_t = row <= col

    def cols(h):
        return pl.ds(h * HEAD, HEAD)

    def put_state(i, h, value):
        per = HEAD // slice_rows
        part[i, h * per:(h + 1) * per] = value.reshape(per, slice_rows, HEAD)

    def state_of(i, h):
        per = HEAD // slice_rows
        return scan_out[i, h * per:(h + 1) * per].reshape(HEAD, HEAD).astype(BF16)

    loads[0].wait()
    loads[1].wait()
    v_t[...] = v[...].T
    for h in range(heads):
        put_state(0, h, dot(v_t[cols(h), :], k[:, cols(h)]))
    loads[2].wait()
    q_t[...] = (q[...].astype(F32) * factor).astype(BF16).T
    loads[3].wait()

    pl.semaphore_wait(barrier, (GROUP - 1) + (n_groups - 1) + (n_tp - 1))

    def to_members(i, src, dst, send, recv):
        copies = []
        for step in STEPS:
            peer = member_at(step)
            copy = pltpu.make_async_remote_copy(
                src_ref=src.at[i, peer],
                dst_ref=dst.at[i, member],
                send_sem=send.at[i],
                recv_sem=recv.at[i],
                device_id=(group * GROUP + peer, tp),
                device_id_type=MESH,
            )
            copy.start()
            copies.append(copy)
        dst[i, pl.ds(member, 1)] = src[i, pl.ds(member, 1)]

    def members_all(i, src, dst, send, recv):
        most = pl.ds(0, GROUP - 1)
        return pltpu.make_async_remote_copy(
            src_ref=src.at[i, most],
            dst_ref=dst.at[i, most],
            send_sem=send.at[i],
            recv_sem=recv.at[i],
            device_id=(ctx, tp),
            device_id_type=MESH,
        )

    def group_copy(i, other):
        return pltpu.make_async_remote_copy(
            src_ref=total.at[i],
            dst_ref=others.at[i, group],
            send_sem=send2.at[i, other],
            recv_sem=recv2.at[i, group],
            device_id=(other * GROUP + member, tp),
            device_id_type=MESH,
        )

    def group_wait(i, other):
        return pltpu.make_async_remote_copy(
            src_ref=total.at[i],
            dst_ref=others.at[i, other],
            send_sem=send2.at[i, other],
            recv_sem=recv2.at[i, other],
            device_id=(other * GROUP + member, tp),
            device_id_type=MESH,
        )

    def scan_start(i):
        to_members(i, part, got, send1, recv1)

    def scan_middle(i):
        members_all(i, part, got, send1, recv1).wait_recv()
        acc = jnp.zeros((slice_rows, HEAD), F32)
        for s in range(GROUP):
            m = s if i == 0 else GROUP - 1 - s
            before[i, m] = acc
            acc = acc + got[i, m]
        total[i] = acc
        for d in range(n_groups - 1, 0, -1):
            other = group + d if i == 0 else group - d

            @pl.when(other < n_groups if i == 0 else other >= 0)
            def _():
                group_copy(i, other).start()

    def scan_end(i):
        for other in range(n_groups):

            @pl.when(other < group if i == 0 else other > group)
            def _():
                group_wait(i, other).wait_recv()

        carried = others[i, 0]
        for other in range(1, n_groups):
            carried = carried + others[i, other]
        before[i] = before[i] + carried[None]
        to_members(i, before, scan_out, send3, recv3)

    def scan_wait(i):
        members_all(i, before, scan_out, send3, recv3).wait_recv()

    scan_start(0)
    w_t[...] = (og[...].astype(F32) * gain_ref[...]).T
    for h in range(heads):
        raw = dot(k[:, cols(h)], q_t[cols(h), :])
        scores_t[h] = jnp.where(causal_t, raw, 0.0).astype(BF16)
    scan_middle(0)
    for h in range(heads):
        local_t[cols(h), :] = dot(v_t[cols(h), :], scores_t[h])
    scan_end(0)
    scan_wait(0)

    power = jnp.zeros((1, tokens), F32)
    row_total = jnp.zeros((1, tokens), F32)
    for h in range(heads):
        att = dot(state_of(0, h), q_t[cols(h), :]) + local_t[cols(h), :]
        att_t[cols(h), :] = att
        power = power + jnp.sum(att * att, axis=0, keepdims=True)
        row_total = row_total + jnp.sum(w_t[cols(h), :] * att, axis=0, keepdims=True)
    rows_out[0:1, :] = power
    rows_out[1:2, :] = row_total

    def tp_copy(d):
        return pltpu.make_async_remote_copy(
            src_ref=rows_out,
            dst_ref=rows_in.at[n_tp - 1 - d],
            send_sem=send_tp.at[d - 1],
            recv_sem=recv_tp.at[n_tp - 1 - d],
            device_id=(ctx, (tp + d) % n_tp),
            device_id_type=MESH,
        )

    for d in range(1, n_tp):
        tp_copy(d).start()
    for d in range(1, n_tp):
        tp_copy(d).wait_recv()
    sums = rows_out[0:2, :]
    for d in range(n_tp - 1):
        sums = sums + rows_in[d, 0:2, :]
    inv = lax.rsqrt(sums[0:1] / features + EPSILON)
    pull = inv * inv * (sums[1:2] / features)
    for h in range(heads):
        ga = (inv * (w_t[cols(h), :] - att_t[cols(h), :] * pull)).astype(BF16)
        ga_t[cols(h), :] = ga
        put_state(1, h, dot(ga, q[:, cols(h)]))
    scan_start(1)

    obuf[0] = ((att_t[...] * inv).T * gain_ref[...]).astype(BF16)
    outs = [
        pltpu.make_async_copy(obuf.at[j], dst, out_sem.at[j])
        for j, dst in enumerate((normed_hbm, gq_hbm, gk_hbm, gv_hbm))
    ]
    outs[0].start()
    for h in range(heads):
        gv_part[:, cols(h)] = dot_t(scores_t[h], ga_t[cols(h), :])
    scan_middle(1)
    for h in range(heads):
        raw = dot(v[:, cols(h)], ga_t[cols(h), :]) * factor
        gs_t = jnp.where(causal_t, raw, 0.0).astype(BF16)
        gk_part[:, cols(h)] = dot(gs_t, q[:, cols(h)])
        gq = dot(ga_t[cols(h), :].T, state_of(0, h)) * factor + dot(gs_t.T, k[:, cols(h)])
        obuf[1, :, cols(h)] = gq.astype(BF16)
    outs[1].start()
    scan_end(1)
    scan_wait(1)
    for h in range(heads):
        s_t = state_of(1, h)
        gk = dot(v[:, cols(h)], s_t) * factor + gk_part[:, cols(h)]
        obuf[2, :, cols(h)] = gk.astype(BF16)
    outs[2].start()
    for h in range(heads):
        s_t = state_of(1, h)
        gv = dot_t(k[:, cols(h)], s_t) * factor + gv_part[:, cols(h)]
        obuf[3, :, cols(h)] = gv.astype(BF16)
    outs[3].start()

    for i in range(2):
        members_all(i, part, got, send1, recv1).wait_send()
        members_all(i, before, scan_out, send3, recv3).wait_send()
        for other in range(n_groups):

            @pl.when(other > group if i == 0 else other < group)
            def _():
                group_wait(i, other).wait_send()

    for d in range(1, n_tp):
        tp_copy(d).wait_send()
    for out in outs:
        out.wait()


def on_device(n_ctx, n_tp, queries, keys, values, gain, out_grad):
    tokens, width = queries.shape
    heads = width // HEAD
    n_groups = n_ctx // GROUP
    slice_rows = heads * HEAD // GROUP
    tile = jax.ShapeDtypeStruct((tokens, width), BF16)
    hbm = pl.BlockSpec(memory_space=pl.ANY)
    vmem = pltpu.VMEM
    dma = pltpu.SemaphoreType.DMA
    return pl.pallas_call(
        functools.partial(core_kernel, n_ctx, n_tp),
        out_shape=(tile,) * 4,
        in_specs=[hbm, hbm, hbm, pl.BlockSpec(memory_space=pltpu.VMEM), hbm],
        out_specs=(hbm,) * 4,
        scratch_shapes=[
            vmem((tokens, width), BF16),
            vmem((tokens, width), BF16),
            vmem((tokens, width), BF16),
            vmem((tokens, width), BF16),
            vmem((2, GROUP, slice_rows, HEAD), F32),
            vmem((2, GROUP, slice_rows, HEAD), F32),
            vmem((2, slice_rows, HEAD), F32),
            vmem((2, n_groups, slice_rows, HEAD), F32),
            vmem((2, GROUP, slice_rows, HEAD), F32),
            vmem((2, GROUP, slice_rows, HEAD), F32),
            vmem((8, tokens), F32),
            vmem((n_tp - 1, 8, tokens), F32),
            vmem((width, tokens), BF16),
            vmem((width, tokens), BF16),
            vmem((width, tokens), F32),
            vmem((width, tokens), F32),
            vmem((width, tokens), F32),
            vmem((heads, tokens, tokens), BF16),
            vmem((width, tokens), BF16),
            vmem((tokens, width), F32),
            vmem((tokens, width), F32),
            vmem((4, tokens, width), BF16),
            dma((4,)),
            dma((4,)),
            dma((2,)),
            dma((2,)),
            dma((2, n_groups)),
            dma((2, n_groups)),
            dma((2,)),
            dma((2,)),
            dma((n_tp - 1,)),
            dma((n_tp - 1,)),
        ],
        compiler_params=pltpu.CompilerParams(
            collective_id=0, has_side_effects=True, vmem_limit_bytes=32 * 1024 * 1024
        ),
        name="linear_attention",
    )(queries, keys, values, gain.reshape(1, width), out_grad)


def solution(mesh):
    placed = (P("ctx", "tp"), P("ctx", "tp"), P("ctx", "tp"), P("tp"), P("ctx", "tp"))
    return jax.shard_map(
        functools.partial(on_device, mesh.shape["ctx"], mesh.shape["tp"]),
        mesh=mesh,
        in_specs=placed,
        out_specs=(P("ctx", "tp"),) * 4,
        check_vma=False,
    )
```

time: 591 us -> 64.3 us (0.11)
  waiting for transfers between devices: 430 us -> 0 us
  other arithmetic: 120 us -> 0 us
  Pallas kernels: 0 us -> 56.5 us
  between operations: 14.2 us -> 0.65 us
  blocking collectives: 8.51 us -> 0 us
    all_gather x2 -> x0, waiting for transfers between devices: 430 us -> none  [carried_in(): gathered = lax.all_gather(part, axis)]
    add x127 -> x0, other arithmetic: 119 us -> none  [add_terms(): return earlier + later]
    pallas_call x0 -> x1, Pallas kernels: none -> 56.5 us  [on_device(): pl.pallas_call(functools.partial(core_kernel, n_ctx, n_tp), out_shape=(ti...]
    psum x1 -> x0, blocking collectives: 8.51 us -> none  [on_device(): power = lax.psum(jnp.sum(attended * attended, axis=(1, 2)), 'tp')]
  transfers between devices with their start and end apart: 2 -> 0, of which waited for: 2 -> 0; matrix products, arithmetic and copies ran while one was open for 1% -> 0% of each run, Pallas kernels for 0% -> 0%
where the time goes in v1:
time: 64.3 us; the launch traced here: 64 us
  Pallas kernels  56.5 us (88%)
  local copies, waits for them, and re-layouts  6.91 us (11%)
  between operations  0.65 us (1%)
    pallas_call x1, Pallas kernels, on_device(): pl.pallas_call(functools.partial(core_kernel, n_ctx, n_tp), out_shape=(ti...  56.5 us
    unnamed x14, local copies, waits for them, and re-layouts  6.91 us

profile of v1, /device:TPU:1, one launch (start us, length us, event | category | flops | bytes accessed | tf_op | source)
XLA Modules:
  0.0 64.0 jit_solution(553481844025883082)
XLA Ops:
  0.6 0.0 copy-start.4
  0.6 0.7 %copy-done.4 = f32[256]{0:T(256)S(1)} copy-done((f32[256]{0:T(256)S(1)}, f32[256]{0:T(256)}, u32[]{:S(2)}) %copy-start.4) | copy-done | bytes 1048
  1.3 0.0 copy-start
  1.3 0.9 %copy-done = bf16[256,256]{1,0:T(8,128)(2,1)S(1)} copy-done((bf16[256,256]{1,0:T(8,128)(2,1)S(1)}, bf16[256,256]{1,0:T(8,128)(2,1)}, u32[]{:S(2)}) %copy-start) | copy-done | bytes 131096
  2.2 0.0 copy-start.1
  2.2 0.9 %copy-done.1 = bf16[256,256]{1,0:T(8,128)(2,1)S(1)} copy-done((bf16[256,256]{1,0:T(8,128)(2,1)S(1)}, bf16[256,256]{1,0:T(8,128)(2,1)}, u32[]{:S(2)}) %copy-start.1) | copy-done | bytes 131096
  3.1 0.0 copy-start.2
  3.1 0.9 %copy-done.2 = bf16[256,256]{1,0:T(8,128)(2,1)S(1)} copy-done((bf16[256,256]{1,0:T(8,128)(2,1)S(1)}, bf16[256,256]{1,0:T(8,128)(2,1)}, u32[]{:S(2)}) %copy-start.2) | copy-done | bytes 131096
  4.0 0.0 copy-start.3
  4.0 0.9 %copy-done.3 = bf16[256,256]{1,0:T(8,128)(2,1)S(1)} copy-done((bf16[256,256]{1,0:T(8,128)(2,1)S(1)}, bf16[256,256]{1,0:T(8,128)(2,1)}, u32[]{:S(2)}) %copy-start.3) | copy-done | bytes 131096
  4.9 56.5 %linear_attention.1 = (bf16[256,256]{1,0:T(8,128)(2,1)S(1)}, bf16[256,256]{1,0:T(8,128)(2,1)S(1)}, bf16[256,256]{1,0:T(8,128)(2,1)S(1)}, bf16[256,256]{1,0:T(8,128)(2,1)S(1)}) custom-call(bf16[256,256]{1,0:T(8,128)(2,1)S(1)} %copy-done, bf16[256,256]{1,0:T(8,128)(2,1)S(1)} %copy-done.1, bf16[256,256]{1,0:T(8,128)(2,1)S(1)} %copy-done.2, ...), custom_call_target="tpu_custom_call" | custom-call | tf_op jit(solution)/shard_map/linear_attention/pallas_call | solution.py:284
  61.4 0.7 %copy.13 = bf16[256,256]{1,0:T(8,128)(2,1)} copy(bf16[256,256]{1,0:T(8,128)(2,1)S(1)} %get-tuple-element.8) | data formatting | bytes 262144
  62.1 0.7 %copy.14 = bf16[256,256]{1,0:T(8,128)(2,1)} copy(bf16[256,256]{1,0:T(8,128)(2,1)S(1)} %get-tuple-element.9) | data formatting | bytes 262144
  62.7 0.7 %copy.15 = bf16[256,256]{1,0:T(8,128)(2,1)} copy(bf16[256,256]{1,0:T(8,128)(2,1)S(1)} %get-tuple-element.10) | data formatting | bytes 262144
  63.4 0.7 %copy.16 = bf16[256,256]{1,0:T(8,128)(2,1)} copy(bf16[256,256]{1,0:T(8,128)(2,1)S(1)} %get-tuple-element.11) | data formatting | bytes 262144
Async XLA Ops:
  0.6 0.7 %copy-start.4 = (f32[256]{0:T(256)S(1)}, f32[256]{0:T(256)}, u32[]{:S(2)}) copy-start(f32[256]{0:T(256)} %param.8) | copy-start | bytes 3076
  1.3 0.9 %copy-start = (bf16[256,256]{1,0:T(8,128)(2,1)S(1)}, bf16[256,256]{1,0:T(8,128)(2,1)}, u32[]{:S(2)}) copy-start(bf16[256,256]{1,0:T(8,128)(2,1)} %q_hbm.1) | copy-start | bytes 393220
  2.2 0.9 %copy-start.1 = (bf16[256,256]{1,0:T(8,128)(2,1)S(1)}, bf16[256,256]{1,0:T(8,128)(2,1)}, u32[]{:S(2)}) copy-start(bf16[256,256]{1,0:T(8,128)(2,1)} %k_hbm.1) | copy-start | bytes 393220
  3.1 0.9 %copy-start.2 = (bf16[256,256]{1,0:T(8,128)(2,1)S(1)}, bf16[256,256]{1,0:T(8,128)(2,1)}, u32[]{:S(2)}) copy-start(bf16[256,256]{1,0:T(8,128)(2,1)} %v_hbm.1) | copy-start | bytes 393220
  4.0 0.9 %copy-start.3 = (bf16[256,256]{1,0:T(8,128)(2,1)S(1)}, bf16[256,256]{1,0:T(8,128)(2,1)}, u32[]{:S(2)}) copy-start(bf16[256,256]{1,0:T(8,128)(2,1)} %og_hbm.1) | copy-start | bytes 393220

commit v2 on v1

--- a/solution.py
+++ b/solution.py
@@ -30,14 +30,13 @@
 
 def core_kernel(
     n_ctx, n_tp,
-    q_hbm, k_hbm, v_hbm, gain_ref, og_hbm,
-    normed_hbm, gq_hbm, gk_hbm, gv_hbm,
-    q, k, v, og,
+    q_hbm, k_hbm, v_hbm, gain_hbm, og_hbm,
+    normed, gq_out, gk_part, gv_part, k_out, v_out, suffix_out,
+    q, k, v, og, gain,
     part, got, total, others, before, scan_out,
     rows_out, rows_in,
     q_t, v_t, w_t, local_t, att_t, scores_t, ga_t,
-    gk_part, gv_part, obuf,
-    in_sem, out_sem, send1, recv1, send2, recv2, send3, recv3, send_tp, recv_tp,
+    in_sem, near_sem, send1, recv1, send2, recv2, send3, recv3, send_tp, recv_tp,
 ):
     ctx = lax.axis_index("ctx")
     tp = lax.axis_index("tp")
@@ -51,11 +50,9 @@
     factor = (HEAD * tokens * n_ctx) ** (-0.5)
     features = width * n_tp
 
-    loads = [
-        pltpu.make_async_copy(src, dst, in_sem.at[i])
-        for i, (src, dst) in enumerate(((k_hbm, k), (v_hbm, v), (q_hbm, q), (og_hbm, og)))
-    ]
-    for load in loads:
+    pairs = ((k_hbm, k), (v_hbm, v), (q_hbm, q), (og_hbm, og), (gain_hbm, gain))
+    loads = [pltpu.make_async_copy(src, dst, in_sem.at[i]) for i, (src, dst) in enumerate(pairs)]
+    for load in loads[:2]:
         load.start()
     others[...] = jnp.zeros_like(others)
 
@@ -64,7 +61,8 @@
         return ((half + dz) % 2) * 8 + ((x + dx) % 4) * 2 + (core + dc) % 2
 
     barrier = pltpu.get_barrier_semaphore()
-    for d in range(1, n_groups):
+    greeted = (2, n_groups - 2, 1, n_groups - 1)
+    for d in greeted:
         pl.semaphore_signal(
             barrier, inc=1, device_id=(((group + d) % n_groups) * GROUP + member, tp), device_id_type=MESH
         )
@@ -75,6 +73,9 @@
     for d in range(1, n_tp):
         pl.semaphore_signal(barrier, inc=1, device_id=(ctx, (tp + d) % n_tp), device_id_type=MESH)
 
+    for load in loads[2:]:
+        load.start()
+
     row = lax.broadcasted_iota(jnp.int32, (tokens, tokens), 0)
     col = lax.broadcasted_iota(jnp.int32, (tokens, tokens), 1)
     causal_t = row <= col
@@ -97,9 +98,12 @@
         put_state(0, h, dot(v_t[cols(h), :], k[:, cols(h)]))
     loads[2].wait()
     q_t[...] = (q[...].astype(F32) * factor).astype(BF16).T
-    loads[3].wait()
-
-    pl.semaphore_wait(barrier, (GROUP - 1) + (n_groups - 1) + (n_tp - 1))
+
+    pl.semaphore_wait(barrier, (GROUP - 1) + len(greeted) + (n_tp - 1))
+    for d in greeted[:2]:
+        pl.semaphore_signal(
+            near_sem, inc=1, device_id=(((group + d) % n_groups) * GROUP + member, tp), device_id_type=MESH
+        )
 
     def to_members(i, src, dst, send, recv):
         copies = []
@@ -183,10 +187,13 @@
         members_all(i, before, scan_out, send3, recv3).wait_recv()
 
     scan_start(0)
-    w_t[...] = (og[...].astype(F32) * gain_ref[...]).T
+    loads[3].wait()
+    loads[4].wait()
+    w_t[...] = (og[...].astype(F32) * gain[...]).T
     for h in range(heads):
         raw = dot(k[:, cols(h)], q_t[cols(h), :])
         scores_t[h] = jnp.where(causal_t, raw, 0.0).astype(BF16)
+    pl.semaphore_wait(near_sem, 2)
     scan_middle(0)
     for h in range(heads):
         local_t[cols(h), :] = dot(v_t[cols(h), :], scores_t[h])
@@ -228,12 +235,7 @@
         put_state(1, h, dot(ga, q[:, cols(h)]))
     scan_start(1)
 
-    obuf[0] = ((att_t[...] * inv).T * gain_ref[...]).astype(BF16)
-    outs = [
-        pltpu.make_async_copy(obuf.at[j], dst, out_sem.at[j])
-        for j, dst in enumerate((normed_hbm, gq_hbm, gk_hbm, gv_hbm))
-    ]
-    outs[0].start()
+    normed[...] = ((att_t[...] * inv).T * gain[...]).astype(BF16)
     for h in range(heads):
         gv_part[:, cols(h)] = dot_t(scores_t[h], ga_t[cols(h), :])
     scan_middle(1)
@@ -242,20 +244,13 @@
         gs_t = jnp.where(causal_t, raw, 0.0).astype(BF16)
         gk_part[:, cols(h)] = dot(gs_t, q[:, cols(h)])
         gq = dot(ga_t[cols(h), :].T, state_of(0, h)) * factor + dot(gs_t.T, k[:, cols(h)])
-        obuf[1, :, cols(h)] = gq.astype(BF16)
-    outs[1].start()
+        gq_out[:, cols(h)] = gq.astype(BF16)
+    k_out[...] = (k[...].astype(F32) * factor).astype(BF16)
+    v_out[...] = (v[...].astype(F32) * factor).astype(BF16)
     scan_end(1)
     scan_wait(1)
     for h in range(heads):
-        s_t = state_of(1, h)
-        gk = dot(v[:, cols(h)], s_t) * factor + gk_part[:, cols(h)]
-        obuf[2, :, cols(h)] = gk.astype(BF16)
-    outs[2].start()
-    for h in range(heads):
-        s_t = state_of(1, h)
-        gv = dot_t(k[:, cols(h)], s_t) * factor + gv_part[:, cols(h)]
-        obuf[3, :, cols(h)] = gv.astype(BF16)
-    outs[3].start()
+        suffix_out[h * HEAD:(h + 1) * HEAD, :] = state_of(1, h)
 
     for i in range(2):
         members_all(i, part, got, send1, recv1).wait_send()
@@ -268,6 +263,28 @@
 
     for d in range(1, n_tp):
         tp_copy(d).wait_send()
+
+
+def last_kernel(
+    normed, gq, gk_part, gv_part, k, v, suffix,
+    normed_hbm, gq_hbm, gk_hbm, gv_hbm,
+    gk, gv, sem,
+):
+    heads = suffix.shape[0] // HEAD
+    outs = [
+        pltpu.make_async_copy(src, dst, sem.at[j])
+        for j, (src, dst) in enumerate(((normed, normed_hbm), (gq, gq_hbm), (gk, gk_hbm), (gv, gv_hbm)))
+    ]
+    outs[0].start()
+    outs[1].start()
+    for h in range(heads):
+        cols = pl.ds(h * HEAD, HEAD)
+        gk[:, cols] = (dot(v[:, cols], suffix[cols, :]) + gk_part[:, cols]).astype(BF16)
+    outs[2].start()
+    for h in range(heads):
+        cols = pl.ds(h * HEAD, HEAD)
+        gv[:, cols] = (dot_t(k[:, cols], suffix[cols, :]) + gv_part[:, cols]).astype(BF16)
+    outs[3].start()
     for out in outs:
         out.wait()
 
@@ -277,20 +294,27 @@
     heads = width // HEAD
     n_groups = n_ctx // GROUP
     slice_rows = heads * HEAD // GROUP
-    tile = jax.ShapeDtypeStruct((tokens, width), BF16)
     hbm = pl.BlockSpec(memory_space=pl.ANY)
+    inside = pl.BlockSpec(memory_space=pltpu.VMEM)
     vmem = pltpu.VMEM
     dma = pltpu.SemaphoreType.DMA
-    return pl.pallas_call(
+    args = [
+        pltpu.with_memory_space_constraint(a, pltpu.HBM)
+        for a in (queries, keys, values, gain.reshape(1, width), out_grad)
+    ]
+    half = pltpu.VMEM((tokens, width), BF16)
+    full = pltpu.VMEM((tokens, width), F32)
+    held = pl.pallas_call(
         functools.partial(core_kernel, n_ctx, n_tp),
-        out_shape=(tile,) * 4,
-        in_specs=[hbm, hbm, hbm, pl.BlockSpec(memory_space=pltpu.VMEM), hbm],
-        out_specs=(hbm,) * 4,
+        out_shape=(half, half, full, full, half, half, pltpu.VMEM((width, HEAD), BF16)),
+        in_specs=[hbm] * 5,
+        out_specs=(inside,) * 7,
         scratch_shapes=[
             vmem((tokens, width), BF16),
             vmem((tokens, width), BF16),
             vmem((tokens, width), BF16),
             vmem((tokens, width), BF16),
+            vmem((1, width), F32),
             vmem((2, GROUP, slice_rows, HEAD), F32),
             vmem((2, GROUP, slice_rows, HEAD), F32),
             vmem((2, slice_rows, HEAD), F32),
@@ -306,11 +330,8 @@
             vmem((width, tokens), F32),
             vmem((heads, tokens, tokens), BF16),
             vmem((width, tokens), BF16),
-            vmem((tokens, width), F32),
-            vmem((tokens, width), F32),
-            vmem((4, tokens, width), BF16),
-            dma((4,)),
-            dma((4,)),
+            dma((5,)),
+            pltpu.SemaphoreType.REGULAR,
             dma((2,)),
             dma((2,)),
             dma((2, n_groups)),
@@ -324,7 +345,21 @@
             collective_id=0, has_side_effects=True, vmem_limit_bytes=32 * 1024 * 1024
         ),
         name="linear_attention",
-    )(queries, keys, values, gain.reshape(1, width), out_grad)
+    )(*args)
+    held = [pltpu.with_memory_space_constraint(a, pltpu.VMEM) for a in held]
+    return pl.pallas_call(
+        last_kernel,
+        out_shape=(pltpu.HBM((tokens, width), BF16),) * 4,
+        in_specs=[inside] * 7,
+        out_specs=(hbm,) * 4,
+        scratch_shapes=[
+            vmem((tokens, width), BF16),
+            vmem((tokens, width), BF16),
+            dma((4,)),
+        ],
+        compiler_params=pltpu.CompilerParams(vmem_limit_bytes=16 * 1024 * 1024),
+        name="last_products",
+    )(*held)
 
 
 def solution(mesh):

time: 64.3 us -> 52.6 us (0.82)
  local copies, waits for them, and re-layouts: 6.91 us -> 0 us
  Pallas kernels: 56.5 us -> 51.8 us
    unnamed x14 -> x0, local copies, waits for them, and re-layouts: 6.91 us -> none
    pallas_call x1 -> x2, Pallas kernels: 56.5 us -> 51.8 us  [the longest x1 50.9 us: on_device(): pl.pallas_call(functools.partial(core_kernel, n_ctx, n_tp), out_shape=(ha...]
where the time goes in v2:
time: 52.6 us; the launch traced here: 52.5 us
  Pallas kernels  51.8 us (98%)
  between operations  0.64 us (1%)
    pallas_call x1, Pallas kernels, on_device(): pl.pallas_call(functools.partial(core_kernel, n_ctx, n_tp), out_shape=(ha...  50.9 us

profile of v2, /device:TPU:1, one launch (start us, length us, event | category | flops | bytes accessed | tf_op | source)
XLA Modules:
  0.0 52.5 jit_solution(11957828899075181780)
XLA Ops:
  0.6 50.9 %linear_attention.1 = (bf16[256,256]{1,0:T(8,128)(2,1)S(1)}, bf16[256,256]{1,0:T(8,128)(2,1)S(1)}, f32[256,256]{1,0:T(8,128)S(1)}, f32[256,256]{1,0:T(8,128)S(1)...) custom-call(bf16[256,256]{1,0:T(8,128)(2,1)} %q_hbm.1, ...), custom_call_target="tpu_custom_call" | custom-call | tf_op jit(solution)/shard_map/linear_attention/pallas_call | solution.py:307
  51.6 0.9 %last_products.1 = (bf16[256,256]{1,0:T(8,128)(2,1)}, bf16[256,256]{1,0:T(8,128)(2,1)}, bf16[256,256]{1,0:T(8,128)(2,1)}, bf16[256,256]{1,0:T(8,128)(2,1)}) custom-call(bf16[256,256]{1,0:T(8,128)(2,1)S(1)} %get-tuple-element.11.normed, bf16[256,256]{1,0:T(8,128)(2,1)S(1)} %get-tuple-element.12.gq, f32[256,256]{1,0:T(8,128)S(1)} %get-tuple-element.13.gk_part, ...), custom_call_target="tpu_custom_call" | custom-call | tf_op jit(solution)/shard_map/last_products/pallas_call | solution.py:350
